TPU v7x, 32 devices: a whole 2x2x4 slice. The times are simulated.
32 devices in a mesh: blk: 16 (over z, y, core), dp: 2 (over x).
Axes of the slice: x: 2, y: 2, z: 4, core: 2. Of those that a mesh axis runs over, the one named last changes fastest.
Arguments:
- image_embed: bfloat16 [24576, 1152], P(('dp', 'blk')), parts along dimension 0, may hold values from -6 to 6
- text_embed: bfloat16 [24576, 1152], P(('dp', 'blk')), parts along dimension 0, may hold values from -6 to 6
- logit_scale: float32 [1], replicated, may hold values from 8 to 20
- logit_bias: float32 [1], replicated, may hold values from -1.5 to 0.5
Outputs:
- row_loss: float32 [24576], P(('dp', 'blk')), parts along dimension 0
- grad_image: float32 [24576, 1152], P(('dp', 'blk')), parts along dimension 0
- grad_text: float32 [24576, 1152], P(('dp', 'blk')), parts along dimension 0
There are 2 independent parts, one for each index of `dp`. A program takes and returns all parts, laid end to end along the dimension named above; an argument that names none is the same for every part. Nothing has to cross between parts.
All inputs are finite; a program needn't handle non-finite values.
Results may differ from a plain program's by a relative error of at most 0.0046.
Values may be sent and summed in bfloat16 or wider, within the bound.
A program may use at most 64 MiB of HBM per device.

v0:
```python
import jax
import jax.numpy as jnp
from jax import lax
from jax.sharding import PartitionSpec as P

EPS = 1e-06


def from_behind(value, axis, steps):
    count = lax.axis_size(axis)
    pairs = [(source, (source + steps) % count) for source in range(count)]
    return lax.ppermute(value, axis, pairs)


def normalize(x):
    xf = x.astype(jnp.float32)
    inv = lax.rsqrt(jnp.sum(xf * xf, axis=-1, keepdims=True) + EPS)
    return (xf * inv, inv)


def unnormalize(unit, inv, grad):
    return inv * (grad - unit * jnp.sum(unit * grad, axis=-1, keepdims=True))


def tile_coef(left, right, scale, bias, sign):
    logits = (
        scale
        * lax.dot_general(left, right, (((1,), (1,)), ((), ())), preferred_element_type=jnp.float32)
        + bias
    )
    losses = jnp.sum(jax.nn.softplus(-sign * logits), axis=1)
    coef = (-scale * sign * jax.nn.sigmoid(-sign * logits)).astype(jnp.bfloat16)
    return (losses, coef)


def image_side(coef, right):
    return jnp.dot(coef, right, preferred_element_type=jnp.float32)


def text_side(coef, left):
    return lax.dot_general(coef, left, (((0,), (0,)), ((), ())), preferred_element_type=jnp.float32)


def shards(image_embed, text_embed, logit_scale, logit_bias):
    scale = logit_scale[0]
    bias = logit_bias[0]
    rows_here = image_embed.shape[0]
    img_unit, inv_img = normalize(image_embed)
    txt_unit, inv_txt = normalize(text_embed)
    img_low = img_unit.astype(jnp.bfloat16)
    txt_low = txt_unit.astype(jnp.bfloat16)
    foreign = []
    current = txt_low
    for step in range(2):
        current = from_behind(current, "blk", 1)
        foreign.append(current)
    positions = lax.iota(jnp.int32, rows_here)
    diag_sign = jnp.where(positions[:, None] == positions[None, :], 1.0, -1.0).astype(jnp.float32)
    total_loss, coef_own = tile_coef(img_low, txt_low, scale, bias, diag_sign)
    loss_one, coef_one = tile_coef(img_low, foreign[0], scale, bias, jnp.float32(-1.0))
    loss_two, coef_two = tile_coef(img_low, foreign[1], scale, bias, jnp.float32(-1.0))
    total_loss = total_loss + loss_one + loss_two
    g_img = (
        image_side(coef_own, txt_low)
        + image_side(coef_one, foreign[0])
        + image_side(coef_two, foreign[1])
    )
    term_own = text_side(coef_own, img_low)
    term_one = text_side(coef_one, img_low)
    term_two = text_side(coef_two, img_low)
    carried = term_two
    for partial_term in (term_one, term_own):
        carried = from_behind(carried, "blk", -1) + partial_term
    row_loss = total_loss / (3 * rows_here)
    grad_image = unnormalize(img_unit, inv_img, g_img)
    grad_text = unnormalize(txt_unit, inv_txt, carried)
    return (row_loss, grad_image, grad_text)


def solution(mesh):
    in_specs = (P(("dp", "blk"), None), P(("dp", "blk"), None), P(), P())
    out_specs = (P(("dp", "blk")), P(("dp", "blk"), None), P(("dp", "blk"), None))
    return jax.shard_map(shards, mesh=mesh, in_specs=in_specs, out_specs=out_specs, check_vma=False)
```

profile of v0, /device:TPU:0, one launch (start us, length us, event | category | flops | bytes accessed | tf_op | source)
XLA Modules:
  0.0 149.8 jit_solution(6705266268841638650)
XLA Ops:
  0.6 0.0 copy-start
  0.6 0.0 copy-start.1
  0.6 2.0 %fusion.13 = f32[768]{0:T(1024)S(1)} fusion(bf16[768,1152]{1,0:T(8,128)(2,1)} %param.5), kind=kLoop, calls=%fused_computation.23 | loop fusion | flops 2653440 | bytes 1772544 | tf_op jit(solution)/shard_map/reduce_sum | solution.py:17
  2.7 0.0 copy-done
  2.7 0.4 fusion.2
  3.1 0.0 copy-start.2
  3.1 1.2 copy-done.2
  4.3 0.5 collective-permute-start
  4.7 25.3 %collective-permute-done = bf16[768,1152]{1,0:T(8,128)(2,1)} collective-permute-done((bf16[768,1152]{1,0:T(8,128)(2,1)S(1)}, bf16[768,1152]{1,0:T(8,128)(2,1)}, u32[]{:S(2)}, u32[]{:S(2)}) %collective-permute-start) | collective-permute-done | bytes 1769504 | tf_op jit(solution)/shard_map/ppermute | solution.py:12
  30.0 0.0 collective-permute-start.1
  31.4 0.0 copy-done.1
  31.4 0.4 fusion.9
  31.8 23.2 %collective-permute-done.1 = bf16[768,1152]{1,0:T(8,128)(2,1)} collective-permute-done((bf16[768,1152]{1,0:T(8,128)(2,1)}, bf16[768,1152]{1,0:T(8,128)(2,1)}, u32[]{:S(2)}, u32[]{:S(2)}) %collective-permute-start.1) | collective-permute-done | bytes 1769504 | tf_op jit(solution)/shard_map/ppermute | solution.py:12
  55.0 4.3 %fusion.19 = (f32[768]{0:T(1024)S(1)}, f32[768,768]{0,1:T(8,128)S(1)}) fusion(f32[]{:T(128)} %bitcast.17, f32[]{:T(128)} %bitcast.10, bf16[768,1152]{1,0:T(8,128)(2,1)} %collective-permute-done.1, bf16[768,1152]{1,0:T(8,128)(2,1)S(1)} %copy-done.1, f32[768]{0:T(1024)S(1)} %add_rsqrt_fusion.1), kind=kOutput, calls=%fused_computation.31 | convolution fusion | flops 1366916352 | bytes 5904392 | tf_op jit(solution)/shard_map/dot_general | solution.py:28
  59.3 0.0 copy-start.3
  59.3 2.2 %fusion.20 = f32[768,1152]{1,0:T(8,128)S(1)} fusion(f32[768,768]{0,1:T(8,128)S(1)} %get-tuple-element.6, f32[]{:T(128)S(6)} %mul.111, f32[]{:T(128)} %bitcast.22, f32[]{:T(128)} %bitcast.15, bf16[768,1152]{1,0:T(8,128)(2,1)S(1)} %copy-done.1, f32[768]{0:T(1024)S(1)} %add_rsqrt_fusion.1), kind=kOutput, calls=%fused_computation.40 | convolution fusion | flops 1365737472 | bytes 7670796 | tf_op jit(solution)/shard_map/dot_general | solution.py:41
  61.4 0.2 collective-permute-start.2
  61.7 0.0 copy-done.3
  61.7 2.9 %fusion.17 = (f32[768]{0:T(1024)S(1)}, f32[768,768]{0,1:T(8,128)S(1)}) fusion(f32[]{:T(128)} %bitcast.16, bf16[768,1152]{1,0:T(8,128)(2,1)S(1)} %copy-done.3, bf16[768,1152]{1,0:T(8,128)(2,1)S(1)} %copy-done.1, f32[768]{0:T(1024)S(1)} %add_rsqrt_fusion.1, f32[]{:T(128)} %bitcast.8), kind=kOutput, calls=%fused_computation.29 | convolution fusion | flops 1369275648 | bytes 5904392 | tf_op jit(solution)/shard_map/dot_general | solution.py:28
  64.6 4.3 %fusion.18 = (f32[768]{0:T(1024)S(1)}, f32[768,768]{0,1:T(8,128)S(1)}) fusion(f32[]{:T(128)} %bitcast.18, f32[]{:T(128)} %bitcast.11, bf16[768,1152]{1,0:T(8,128)(2,1)} %collective-permute-done, bf16[768,1152]{1,0:T(8,128)(2,1)S(1)} %copy-done.1, f32[768]{0:T(1024)S(1)} %add_rsqrt_fusion.1), kind=kOutput, calls=%fused_computation.30 | convolution fusion | flops 1366916352 | bytes 5904392 | tf_op jit(solution)/shard_map/dot_general | solution.py:28
  68.8 31.9 %collective-permute-done.2 = f32[768,1152]{1,0:T(8,128)S(1)} collective-permute-done((f32[768,1152]{1,0:T(8,128)S(1)}, f32[768,1152]{1,0:T(8,128)S(1)}, u32[]{:S(2)}, u32[]{:S(2)}) %collective-permute-start.2) | collective-permute-done | bytes 3538976 | tf_op jit(solution)/shard_map/ppermute | solution.py:12
  100.7 2.0 %convolution_add_fusion = f32[768,1152]{1,0:T(8,128)S(1)} fusion(f32[768,1152]{1,0:T(8,128)S(1)} %collective-permute-done.2, f32[768,768]{0,1:T(8,128)S(1)} %get-tuple-element.10, f32[]{:T(128)S(6)} %mul.111, f32[]{:T(128)} %bitcast.21, f32[]{:T(128)} %bitcast.14, bf16[768,1152]{1,0:T(8,128)(2,1)S(1)} %copy-done.1, f32[768]{0:T(1024)S(1)} %add_rsqrt_fusion.1), kind=kOutput, calls=%fused_computation.13 | convolution fusion | flops 1366622208 | bytes 11209740 | tf_op jit(solution)/shard_map/dot_general | solution.py:41
  102.7 4.9 %collective-permute-start.3 = (f32[768,1152]{1,0:T(8,128)S(1)}, f32[768,1152]{1,0:T(8,128)S(1)}, u32[]{:S(2)}, u32[]{:S(2)}) collective-permute-start(f32[768,1152]{1,0:T(8,128)S(1)} %convolution_add_fusion), channel_id=1, source_target_pairs={{0,30},{2,0},{4,2},{6,4},{8,6},{10,8},{12,10},{14,12},{16,14},{18,... | collective-permute-start | bytes 10616840 | tf_op jit(solution)/shard_map/ppermute | solution.py:12
  107.6 1.8 %fusion.23 = f32[768,1152]{1,0:T(8,128)S(1)} fusion(bf16[768,1152]{1,0:T(8,128)(2,1)S(1)} %copy-done.3, f32[768,768]{0,1:T(8,128)S(1)} %get-tuple-element.8, f32[]{:T(128)S(6)} %neg.32), kind=kOutput, calls=%fused_computation.42 | convolution fusion | flops 1363673088 | bytes 7667716 | tf_op jit(solution)/shard_map/dot_general | solution.py:37
  109.4 2.1 %fusion.21 = f32[768,1152]{1,0:T(8,128)S(1)} fusion(f32[768,768]{0,1:T(8,128)S(1)} %get-tuple-element.8, f32[]{:T(128)S(6)} %neg.32, bf16[768,1152]{1,0:T(8,128)(2,1)S(1)} %copy-done.1, f32[768]{0:T(1024)S(1)} %add_rsqrt_fusion.1), kind=kOutput, calls=%fused_computation.41 | convolution fusion | flops 1366327296 | bytes 7670788 | tf_op jit(solution)/shard_map/dot_general | solution.py:41
  111.5 3.4 %convolution_add_fusion.2 = f32[768,1152]{1,0:T(8,128)S(1)} fusion(f32[768,1152]{1,0:T(8,128)S(1)} %fusion.23, bf16[768,1152]{1,0:T(8,128)(2,1)} %collective-permute-done, f32[768,768]{0,1:T(8,128)S(1)} %get-tuple-element.10, f32[]{:T(128)S(6)} %mul.111, f32[]{:T(128)} %bitcast.20, f32[]{:T(128)} %bitcast.13), kind=kOutput, calls=%fused_computation.15 | convolution fusion | flops 1363968000 | bytes 11206668 | tf_op jit(solution)/shard_map/dot_general | solution.py:37
  115.0 0.6 add_multiply_fusion
  115.5 3.8 %fusion.6 = (f32[768]{0:T(1024)S(1)}, f32[768,1152]{1,0:T(8,128)S(1)}) fusion(bf16[768,1152]{1,0:T(8,128)(2,1)S(1)} %copy-done.1, f32[768]{0:T(1024)S(1)} %add_rsqrt_fusion.1, f32[768,1152]{1,0:T(8,128)S(1)} %convolution_add_fusion.2, bf16[768,1152]{1,0:T(8,128)(2,1)} %collective-permute-done.1, f32[768,768]{0,1:T(8,128)S(1)} %get-tuple-element.6, ...), kind=kOutput, calls=%fused_computation.16 | convolution fusion | flops 1367506176 | bytes 12982284 | tf_op jit(solution)/shard_map/dot_general | solution.py:37
  119.4 2.5 %fusion.8 = f32[768,1152]{1,0:T(8,128)} fusion(f32[768,1152]{1,0:T(8,128)S(1)} %get-tuple-element.12, bf16[768,1152]{1,0:T(8,128)(2,1)S(1)} %copy-done.1, f32[768]{0:T(1024)S(1)} %get-tuple-element.11, f32[768]{0:T(1024)S(1)} %add_rsqrt_fusion.1), kind=kLoop, calls=%fused_computation.18 | loop fusion | flops 4423680 | bytes 8853504 | tf_op jit(solution)/shard_map/mul | solution.py:22
  121.8 24.7 %collective-permute-done.3 = f32[768,1152]{1,0:T(8,128)S(1)} collective-permute-done((f32[768,1152]{1,0:T(8,128)S(1)}, f32[768,1152]{1,0:T(8,128)S(1)}, u32[]{:S(2)}, u32[]{:S(2)}) %collective-permute-start.3) | collective-permute-done | bytes 3538976 | tf_op jit(solution)/shard_map/ppermute | solution.py:12
  146.6 0.8 fusion.10
  147.4 2.5 %fusion.12 = f32[768,1152]{1,0:T(8,128)} fusion(f32[768,1152]{1,0:T(8,128)S(1)} %get-tuple-element.4, bf16[768,1152]{1,0:T(8,128)(2,1)S(1)} %copy-done, f32[768]{0:T(1024)S(1)} %get-tuple-element.3, f32[768]{0:T(1024)S(1)} %add_rsqrt_fusion), kind=kLoop, calls=%fused_computation.22 | loop fusion | flops 4423680 | bytes 8853504 | tf_op jit(solution)/shard_map/mul | solution.py:22
  (2 shorter events, 0.0 us)
Async XLA Ops:
  0.6 2.1 %copy-start = (bf16[768,1152]{1,0:T(8,128)(2,1)S(1)}, bf16[768,1152]{1,0:T(8,128)(2,1)}, u32[]{:S(2)}) copy-start(bf16[768,1152]{1,0:T(8,128)(2,1)} %param.5) | copy-start | bytes 5308420
  0.6 30.7 %copy-start.1 = (bf16[768,1152]{1,0:T(8,128)(2,1)S(1)}, bf16[768,1152]{1,0:T(8,128)(2,1)}, u32[]{:S(2)}) copy-start(bf16[768,1152]{1,0:T(8,128)(2,1)} %param.4) | copy-start | bytes 5308420
  3.1 1.2 copy-start.2
  4.3 25.8 %collective-permute-start = (bf16[768,1152]{1,0:T(8,128)(2,1)S(1)}, bf16[768,1152]{1,0:T(8,128)(2,1)}, u32[]{:S(2)}, u32[]{:S(2)}) collective-permute-start(bf16[768,1152]{1,0:T(8,128)(2,1)S(1)} %fusion.2), channel_id=1, source_target_pairs={{0,2},{2,4},{4,6},{6,8},{8,10},{10,12},{12,14},{14,16},{16,18},{18... | collective-permute-start | bytes 5308424 | tf_op jit(solution)/shard_map/ppermute | solution.py:12
  30.0 25.0 %collective-permute-start.1 = (bf16[768,1152]{1,0:T(8,128)(2,1)}, bf16[768,1152]{1,0:T(8,128)(2,1)}, u32[]{:S(2)}, u32[]{:S(2)}) collective-permute-start(bf16[768,1152]{1,0:T(8,128)(2,1)} %collective-permute-done), channel_id=1, source_target_pairs={{0,2},{2,4},{4,6},{6,8},{8,10},{10,12},{12,14},{14,16},{16,18},{18... | collective-permute-start | bytes 5308424 | tf_op jit(solution)/shard_map/ppermute | solution.py:12
  59.3 2.4 %copy-start.3 = (bf16[768,1152]{1,0:T(8,128)(2,1)S(1)}, bf16[768,1152]{1,0:T(8,128)(2,1)}, u32[]{:S(2)}) copy-start(bf16[768,1152]{1,0:T(8,128)(2,1)} %copy-done.2) | copy-start | bytes 5308420
  61.4 39.2 %collective-permute-start.2 = (f32[768,1152]{1,0:T(8,128)S(1)}, f32[768,1152]{1,0:T(8,128)S(1)}, u32[]{:S(2)}, u32[]{:S(2)}) collective-permute-start(f32[768,1152]{1,0:T(8,128)S(1)} %fusion.20), channel_id=1, source_target_pairs={{0,30},{2,0},{4,2},{6,4},{8,6},{10,8},{12,10},{14,12},{16,14},{18,... | collective-permute-start | bytes 10616840 | tf_op jit(solution)/shard_map/ppermute | solution.py:12
  102.7 43.9 %collective-permute-start.3 = (f32[768,1152]{1,0:T(8,128)S(1)}, f32[768,1152]{1,0:T(8,128)S(1)}, u32[]{:S(2)}, u32[]{:S(2)}) collective-permute-start(f32[768,1152]{1,0:T(8,128)S(1)} %convolution_add_fusion), channel_id=1, source_target_pairs={{0,30},{2,0},{4,2},{6,4},{8,6},{10,8},{12,10},{14,12},{16,14},{18,... | collective-permute-start | bytes 10616840 | tf_op jit(solution)/shard_map/ppermute | solution.py:12
where the time goes:
time: 150 us
  waiting for transfers between devices  105 us (70%)
  matrix products  26.7 us (18%)
  other arithmetic  9.16 us (6%)
  starting transfers between devices  5.57 us (4%)
  between operations  2.07 us (1%)
    ppermute x4, waiting for transfers between devices, from_behind(): return lax.ppermute(value, axis, pairs)  105 us
    dot_general x3, matrix products, tile_coef(): lax.dot_general(left, right, (((1,), (1,)), ((), ())), preferred_element_...  11.4 us
    dot_general x3, matrix products, image_side(): return jnp.dot(coef, right, preferred_element_type=jnp.float32)  9.04 us
    dot_general x3, matrix products, text_side(): lax.dot_general(coef, left, (((0,), (0,)), ((), ())), preferred_element_t...  6.28 us
    ppermute x4, starting transfers between devices, from_behind(): return lax.ppermute(value, axis, pairs)  5.57 us
    mul x2, other arithmetic, unnormalize(): return inv * (grad - unit * jnp.sum(unit * grad, axis=-1, keepdims=True))  4.92 us
  transfers between devices with their start and end apart: 4, of which 4 were waited for; matrix products, arithmetic and copies ran while one was open for 15% of the time, Pallas kernels for 0%

commit v1 on v0

v1 whole, which is shorter than its diff:
```python
import functools

import jax
import jax.numpy as jnp
from jax import lax
from jax.experimental import pallas as pl
from jax.experimental.pallas import tpu as pltpu
from jax.sharding import PartitionSpec as P

EPS = 1e-06
MESH = pl.DeviceIdType.MESH
TXT, IMG = 0, 1


def normalize(x):
    xf = x.astype(jnp.float32)
    inv = lax.rsqrt(jnp.sum(xf * xf, axis=-1, keepdims=True) + EPS)
    return xf * inv, inv


def dot_t(left, right):
    return lax.dot_general(left, right, (((1,), (1,)), ((), ())), preferred_element_type=jnp.float32)


def dot(left, right):
    return jnp.dot(left, right, preferred_element_type=jnp.float32)


def terms(x):
    e = jnp.exp(-jnp.abs(x))
    loss = jnp.maximum(x, 0.0) + jnp.log1p(e)
    sig = jnp.where(x >= 0.0, 1.0, e) / (1.0 + e)
    return loss, sig


def exchange(n, chunk, scale_ref, bias_ref, img_ref, txt_ref, acc, loss,
             low, far, send_sem, recv_sem):
    rows = img_ref.shape[0]
    count = rows // chunk
    me = lax.axis_index("blk")
    parity = lax.rem(me, 2)

    def at(step):
        return {"blk": lax.rem(me + step + n, n)}

    barrier = pltpu.get_barrier_semaphore()
    for step in (1, -1, 2, -2):
        pl.semaphore_signal(barrier, inc=1, device_id=at(step), device_id_type=MESH)

    def make_low(c):
        here = pl.ds(pl.multiple_of(c * chunk, chunk), chunk)
        low[TXT, here, :] = normalize(txt_ref[here, :])[0].astype(jnp.bfloat16)
        low[IMG, here, :] = normalize(img_ref[here, :])[0].astype(jnp.bfloat16)

    def copies(c):
        here = pl.ds(pl.multiple_of(c * chunk, chunk), chunk)

        def copy(src, kind, dist, slot, to):
            return pltpu.make_async_remote_copy(
                src_ref=src, dst_ref=far.at[kind, dist, here, :],
                send_sem=send_sem.at[slot, c], recv_sem=recv_sem.at[kind, dist, c],
                device_id=to, device_id_type=MESH)

        sign = 1 - 2 * parity
        two = at(2 * sign)
        one = at(sign)
        return (
            copy(low.at[parity, here, :], parity, 1, 2, two),
            copy(low.at[TXT, here, :], TXT, 0, 0, at(1)),
            copy(low.at[IMG, here, :], IMG, 0, 1, at(-1)),
            copy(far.at[parity, 0, here, :], parity, 1, 3, one),
        )

    make_low(0)
    pl.semaphore_wait(barrier, 4)

    def start(c, _):
        direct_two, text_one, image_one, _ = copies(c)
        direct_two.start()
        text_one.start()
        image_one.start()

        @pl.when(c + 1 < count)
        def _():
            make_low(c + 1)
        return 0

    lax.fori_loop(0, count, start, 0)

    scale = scale_ref[0]
    bias = bias_ref[0]
    acc[...] = jnp.zeros_like(acc)
    loss[...] = jnp.zeros_like(loss)

    def own(c, _):
        here = pl.ds(pl.multiple_of(c * chunk, chunk), chunk)
        text = low[TXT, here, :]
        logits = scale * dot_t(low[IMG], text) + bias
        row = lax.broadcasted_iota(jnp.int32, logits.shape, 0)
        col = lax.broadcasted_iota(jnp.int32, logits.shape, 1) + c * chunk
        flip = jnp.where(row == col, -1.0, 1.0).astype(jnp.float32)
        part, sig = terms(flip * logits)
        coef = (scale * flip * sig).astype(jnp.bfloat16)
        loss[IMG] += part
        acc[IMG] += dot(coef, text)
        acc[TXT, here, :] = lax.dot_general(
            coef, low[IMG], (((0,), (0,)), ((), ())), preferred_element_type=jnp.float32)
        return 0

    lax.fori_loop(0, count, own, 0)

    def foreign(kind, dist, c):
        here = pl.ds(pl.multiple_of(c * chunk, chunk), chunk)
        block = far[kind, dist, here, :]
        mine = 1 - kind
        part, sig = terms(scale * dot_t(low[mine], block) + bias)
        loss[mine] += part
        acc[mine] += dot((scale * sig).astype(jnp.bfloat16), block)

    def near(c, _):
        _, text_one, image_one, _ = copies(c)

        @pl.when(parity == 0)
        def _():
            image_one.wait_recv()

        @pl.when(parity == 1)
        def _():
            text_one.wait_recv()
        foreign(1 - parity, 0, c)
        return 0

    lax.fori_loop(0, count, near, 0)

    def across(c, _):
        direct_two, text_one, image_one, relay = copies(c)

        @pl.when(parity == 0)
        def _():
            text_one.wait_recv()

        @pl.when(parity == 1)
        def _():
            image_one.wait_recv()
        relay.start()
        foreign(parity, 0, c)
        direct_two.wait_recv()
        foreign(parity, 1, c)
        here = pl.ds(pl.multiple_of(c * chunk, chunk), chunk)
        pltpu.make_async_remote_copy(
            src_ref=far.at[parity, 0, here, :], dst_ref=far.at[1 - parity, 1, here, :],
            send_sem=send_sem.at[3, c], recv_sem=recv_sem.at[1 - parity, 1, c],
            device_id=at(1), device_id_type=MESH).wait_recv()
        foreign(1 - parity, 1, c)
        return 0

    lax.fori_loop(0, count, across, 0)

    def finish(c, _):
        for copy in copies(c):
            copy.wait_send()
        return 0

    lax.fori_loop(0, count, finish, 0)


def unnormalize(img_ref, txt_ref, acc_ref, loss_ref, img_out, txt_out, row_out):
    for kind, x, out in ((IMG, img_ref, img_out), (TXT, txt_ref, txt_out)):
        unit, inv = normalize(x[...])
        g = acc_ref[kind]
        out[...] = inv * (g - unit * jnp.sum(unit * g, axis=-1, keepdims=True))
    row_out[...] = jnp.sum(loss_ref[...].T, axis=0, keepdims=True)[None]


def shards(n, image_embed, text_embed, logit_scale, logit_bias):
    rows, width = image_embed.shape
    chunk = 128
    count = rows // chunk
    vmem = pl.BlockSpec(memory_space=pltpu.VMEM)
    smem = pl.BlockSpec(memory_space=pltpu.SMEM)
    acc, loss = pl.pallas_call(
        functools.partial(exchange, n, chunk),
        out_shape=(jax.ShapeDtypeStruct((2, rows, width), jnp.float32),
                   jax.ShapeDtypeStruct((2, rows, chunk), jnp.float32)),
        in_specs=[smem, smem, vmem, vmem],
        out_specs=(vmem, vmem),
        scratch_shapes=[
            pltpu.VMEM((2, rows, width), jnp.bfloat16),
            pltpu.VMEM((2, 2, rows, width), jnp.bfloat16),
            pltpu.SemaphoreType.DMA((4, count)),
            pltpu.SemaphoreType.DMA((2, 2, count)),
        ],
        compiler_params=pltpu.CompilerParams(
            collective_id=0, has_side_effects=True, vmem_limit_bytes=48 * 2**20),
        cost_estimate=pl.CostEstimate(
            flops=22 * rows * rows * width, bytes_accessed=12 * rows * width,
            transcendentals=10 * rows * rows),
    )(logit_scale, logit_bias, image_embed, text_embed)
    block = pl.BlockSpec((chunk, width), lambda c: (c, 0))
    grad_image, grad_text, row_loss = pl.pallas_call(
        unnormalize,
        grid=(count,),
        out_shape=(jax.ShapeDtypeStruct((rows, width), jnp.float32),
                   jax.ShapeDtypeStruct((rows, width), jnp.float32),
                   jax.ShapeDtypeStruct((count, 1, chunk), jnp.float32)),
        in_specs=[block, block,
                  pl.BlockSpec((2, chunk, width), lambda c: (0, c, 0)),
                  pl.BlockSpec((None, chunk, chunk), lambda c: (IMG, c, 0))],
        out_specs=(block, block, pl.BlockSpec((1, 1, chunk), lambda c: (c, 0, 0))),
        compiler_params=pltpu.CompilerParams(vmem_limit_bytes=32 * 2**20),
    )(image_embed, text_embed, acc, loss)
    return row_loss.reshape(rows) / (3 * rows), grad_image, grad_text


def solution(mesh):
    in_specs = (P(("dp", "blk"), None), P(("dp", "blk"), None), P(), P())
    out_specs = (P(("dp", "blk")), P(("dp", "blk"), None), P(("dp", "blk"), None))
    return jax.shard_map(functools.partial(shards, mesh.shape["blk"]), mesh=mesh,
                         in_specs=in_specs, out_specs=out_specs, check_vma=False)
```

time: 150 us -> 103 us (0.69)
  the two profiles are of different devices: /device:TPU:0 before, /device:TPU:1 now
where the time goes in v1:
time: 103 us
  Pallas kernels  94.3 us (92%)
  local copies, waits for them, and re-layouts  5.95 us (6%)
  between operations  1.95 us (2%)
    pallas_call x1, Pallas kernels, shards(): pl.pallas_call(functools.partial(exchange, n, chunk), out_shape=(jax.Shap...  89.6 us
    unnamed x6, local copies, waits for them, and re-layouts  5.95 us
    pallas_call x1, Pallas kernels, shards(): pl.pallas_call(unnormalize, grid=(count,), out_shape=(jax.ShapeDtypeStruc...  4.69 us

profile of v1, /device:TPU:1, one launch (start us, length us, event | category | flops | bytes accessed | tf_op | source)
XLA Modules:
  0.0 102.8 jit_solution(2871969399193361673)
XLA Ops:
  1.9 0.0 copy-start.1
  1.9 1.5 %copy-done.1 = bf16[768,1152]{1,0:T(8,128)(2,1)S(1)} copy-done((bf16[768,1152]{1,0:T(8,128)(2,1)S(1)}, bf16[768,1152]{1,0:T(8,128)(2,1)}, u32[]{:S(2)}) %copy-start.1) | copy-done | bytes 1769496
  3.4 0.0 copy-start.2
  3.4 1.5 %copy-done.2 = bf16[768,1152]{1,0:T(8,128)(2,1)S(1)} copy-done((bf16[768,1152]{1,0:T(8,128)(2,1)S(1)}, bf16[768,1152]{1,0:T(8,128)(2,1)}, u32[]{:S(2)}) %copy-start.2) | copy-done | bytes 1769496
  4.9 89.6 %shard_map.67 = (f32[2,768,1152]{2,1,0:T(8,128)}, f32[2,768,128]{2,1,0:T(8,128)S(1)}) custom-call(f32[1]{0:T(128)S(6)} %copy.7.scale_ref, f32[1]{0:T(128)S(6)} %copy.8.bias_ref, bf16[768,1152]{1,0:T(8,128)(2,1)S(1)} %copy-done.1, bf16[768,1152]{1,0:T(8,128)(2,1)S(1)} %copy-done.2), custom_call_target="tpu_custom_call" | custom-call | flops 14948499456 | bytes 10616832 | tf_op jit(solution)/shard_map/pallas_call | solution.py:181
  94.5 0.0 copy-start
  94.5 3.0 %copy-done = f32[2,768,1152]{2,1,0:T(8,128)S(1)} copy-done((f32[2,768,1152]{2,1,0:T(8,128)S(1)}, f32[2,768,1152]{2,1,0:T(8,128)}, u32[]{:S(2)}) %copy-start) | copy-done | bytes 7077912
  97.5 4.7 %shard_map.68 = (f32[768,1152]{1,0:T(8,128)}, f32[768,1152]{1,0:T(8,128)}, f32[6,1,128]{2,1,0:T(1,128)S(1)}) custom-call(bf16[768,1152]{1,0:T(8,128)(2,1)S(1)} %copy-done.1, bf16[768,1152]{1,0:T(8,128)(2,1)S(1)} %copy-done.2, f32[2,768,1152]{2,1,0:T(8,128)S(1)} %copy-done, f32[2,768,128]{2,1,0:T(8,128)S(1)} %get-tuple-element.9.loss_ref), custom_call_target="tpu_custom_call" | custom-call | tf_op jit(solution)/shard_map/pallas_call | solution.py:200
  102.2 0.6 multiply_reduce_fusion
Async XLA Ops:
  1.9 1.5 %copy-start.1 = (bf16[768,1152]{1,0:T(8,128)(2,1)S(1)}, bf16[768,1152]{1,0:T(8,128)(2,1)}, u32[]{:S(2)}) copy-start(bf16[768,1152]{1,0:T(8,128)(2,1)} %img_ref.3) | copy-start | bytes 5308420
  3.4 1.5 %copy-start.2 = (bf16[768,1152]{1,0:T(8,128)(2,1)S(1)}, bf16[768,1152]{1,0:T(8,128)(2,1)}, u32[]{:S(2)}) copy-start(bf16[768,1152]{1,0:T(8,128)(2,1)} %txt_ref.3) | copy-start | bytes 5308420
  94.5 3.0 %copy-start = (f32[2,768,1152]{2,1,0:T(8,128)S(1)}, f32[2,768,1152]{2,1,0:T(8,128)}, u32[]{:S(2)}) copy-start(f32[2,768,1152]{2,1,0:T(8,128)} %get-tuple-element.8.acc_ref) | copy-start | bytes 21233668

commit v2 on v1

v2 whole, which is shorter than its diff:
```python
import functools

import jax
import jax.numpy as jnp
from jax import lax
from jax.experimental import pallas as pl
from jax.experimental.pallas import tpu as pltpu
from jax.sharding import PartitionSpec as P

EPS = 1e-06
MESH = pl.DeviceIdType.MESH
TXT, IMG = 0, 1


def normalize(x):
    xf = x.astype(jnp.float32)
    inv = lax.rsqrt(jnp.sum(xf * xf, axis=-1, keepdims=True) + EPS)
    return xf * inv, inv


def dot_t(left, right):
    return lax.dot_general(left, right, (((1,), (1,)), ((), ())), preferred_element_type=jnp.float32)


def dot(left, right):
    return jnp.dot(left, right, preferred_element_type=jnp.float32)


def terms(x):
    e = jnp.exp(-jnp.abs(x))
    loss = jnp.maximum(x, 0.0) + jnp.log1p(e)
    sig = jnp.where(x >= 0.0, 1.0, e) / (1.0 + e)
    return loss, sig


def exchange(n, chunk, scale_ref, bias_ref, img_hbm, txt_hbm, acc, row_out,
             raw, low, far, inverse, loss, load_sem, send_sem, recv_sem):
    rows = raw.shape[1]
    count = rows // chunk
    me = lax.axis_index("blk")
    parity = lax.rem(me, 2)
    sign = 1 - 2 * parity

    def at(step):
        return {"blk": lax.rem(me + step + n, n)}

    def span(c):
        return pl.ds(pl.multiple_of(c * chunk, chunk), chunk)

    def loads(c):
        return [pltpu.make_async_copy(source.at[span(c), :], raw.at[kind, span(c), :], load_sem.at[kind, c])
                for kind, source in ((TXT, txt_hbm), (IMG, img_hbm))]

    def copy(src, kind, dist, slot, c, to):
        return pltpu.make_async_remote_copy(
            src_ref=src, dst_ref=far.at[kind, dist, span(c), :],
            send_sem=send_sem.at[slot, c], recv_sem=recv_sem.at[kind, dist, c],
            device_id=to, device_id_type=MESH)

    def text_one(c):
        return copy(low.at[TXT, span(c), :], TXT, 0, 0, c, at(1))

    def image_one(c):
        return copy(low.at[IMG, span(c), :], IMG, 0, 1, c, at(-1))

    def direct_two(c):
        return copy(low.at[parity, span(c), :], parity, 1, 2, c, at(2 * sign))

    def relay(c):
        return copy(far.at[parity, 0, span(c), :], parity, 1, 3, c, at(sign))

    def arrived(kind, dist, c):
        copy(far.at[kind, dist, span(c), :], kind, dist, 0, c, at(1)).wait_recv()

    def each(body, low_c=0, high_c=count):
        def step(c, carry):
            body(c)
            return carry
        lax.fori_loop(low_c, high_c, step, 0)

    barrier = pltpu.get_barrier_semaphore()
    for step in (1, -1, 2, -2):
        pl.semaphore_signal(barrier, inc=1, device_id=at(step), device_id_type=MESH)

    @each
    def _(c):
        for load in loads(c):
            load.start()

    def make_low(c):
        for load in loads(c):
            load.wait()
        for kind in (TXT, IMG):
            unit, inv = normalize(raw[kind, span(c), :])
            low[kind, span(c), :] = unit.astype(jnp.bfloat16)
            inverse[kind, span(c), :] = inv

    make_low(0)
    pl.semaphore_wait(barrier, 4)

    @each
    def _(c):
        text_one(c).start()
        image_one(c).start()

        @pl.when(c + 1 < count)
        def _():
            make_low(c + 1)

    scale = scale_ref[0]
    bias = bias_ref[0]
    acc[IMG] = jnp.zeros_like(acc[IMG])
    loss[...] = jnp.zeros_like(loss)

    @each
    def _(c):
        text = low[TXT, span(c), :]
        logits = scale * dot_t(low[IMG], text) + bias
        row = lax.broadcasted_iota(jnp.int32, logits.shape, 0)
        col = lax.broadcasted_iota(jnp.int32, logits.shape, 1) + c * chunk
        flip = jnp.where(row == col, -1.0, 1.0).astype(jnp.float32)
        part, sig = terms(flip * logits)
        coef = (scale * flip * sig).astype(jnp.bfloat16)
        loss[IMG] += part
        acc[IMG] += dot(coef, text)
        acc[TXT, span(c), :] = lax.dot_general(
            coef, low[IMG], (((0,), (0,)), ((), ())), preferred_element_type=jnp.float32)

    def foreign(kind, dist, c):
        block = far[kind, dist, span(c), :]
        mine = 1 - kind
        part, sig = terms(scale * dot_t(low[mine], block) + bias)
        loss[mine] += part
        acc[mine] += dot((scale * sig).astype(jnp.bfloat16), block)

    def take(kind, dist, c):
        arrived(kind, dist, c)
        foreign(kind, dist, c)

    def finish(kind):
        @each
        def _(c):
            inv = inverse[kind, span(c), :]
            unit = raw[kind, span(c), :].astype(jnp.float32) * inv
            g = acc[kind, span(c), :]
            acc[kind, span(c), :] = inv * (g - unit * jnp.sum(unit * g, axis=-1, keepdims=True))

    each(lambda c: take(1 - parity, 0, c))

    each(lambda c: direct_two(c).start())
    lag = count // 2

    @each
    def _(c):
        arrived(parity, 0, c)
        relay(c).start()
        foreign(parity, 0, c)

        @pl.when(c >= lag)
        def _():
            take(parity, 1, c - lag)

    each(lambda c: take(1 - parity, 1, c))
    finish(parity)
    each(lambda c: take(parity, 1, c), count - lag)
    finish(1 - parity)

    @each
    def _(c):
        lanes = jnp.sum(loss[IMG, span(c), :].T, axis=0, keepdims=True)
        row_out[c] = lanes / (3 * rows)

    @each
    def _(c):
        for sent in (text_one, image_one, direct_two, relay):
            sent(c).wait_send()


def shards(n, image_embed, text_embed, logit_scale, logit_bias):
    rows, width = image_embed.shape
    chunk = 128
    count = rows // chunk
    vmem = pl.BlockSpec(memory_space=pltpu.VMEM)
    smem = pl.BlockSpec(memory_space=pltpu.SMEM)
    hbm = pl.BlockSpec(memory_space=pltpu.HBM)
    grads, row_loss = pl.pallas_call(
        functools.partial(exchange, n, chunk),
        out_shape=(jax.ShapeDtypeStruct((2, rows, width), jnp.float32),
                   jax.ShapeDtypeStruct((count, 1, chunk), jnp.float32)),
        in_specs=[smem, smem, hbm, hbm],
        out_specs=(vmem, vmem),
        scratch_shapes=[
            pltpu.VMEM((2, rows, width), jnp.bfloat16),
            pltpu.VMEM((2, rows, width), jnp.bfloat16),
            pltpu.VMEM((2, 2, rows, width), jnp.bfloat16),
            pltpu.VMEM((2, rows, 1), jnp.float32),
            pltpu.VMEM((2, rows, chunk), jnp.float32),
            pltpu.SemaphoreType.DMA((2, count)),
            pltpu.SemaphoreType.DMA((4, count)),
            pltpu.SemaphoreType.DMA((2, 2, count)),
        ],
        compiler_params=pltpu.CompilerParams(
            collective_id=0, has_side_effects=True, vmem_limit_bytes=28 * 2**20),
        cost_estimate=pl.CostEstimate(
            flops=22 * rows * rows * width, bytes_accessed=12 * rows * width,
            transcendentals=10 * rows * rows),
    )(logit_scale, logit_bias, image_embed, text_embed)
    return row_loss.reshape(rows), grads[IMG], grads[TXT]


def solution(mesh):
    in_specs = (P(("dp", "blk"), None), P(("dp", "blk"), None), P(), P())
    out_specs = (P(("dp", "blk")), P(("dp", "blk"), None), P(("dp", "blk"), None))
    return jax.shard_map(functools.partial(shards, mesh.shape["blk"]), mesh=mesh,
                         in_specs=in_specs, out_specs=out_specs, check_vma=False)
```

time: 103 us -> 109 us (1.058)
  Pallas kernels: 94.3 us -> 99.5 us
    pallas_call x1, Pallas kernels: 89.6 us -> 99.5 us  [shards(): pl.pallas_call(functools.partial(exchange, n, chunk), out_shape=(jax.Shap...]
    pallas_call x1 -> x0, Pallas kernels: 4.69 us -> none  [shards(): pl.pallas_call(unnormalize, grid=(count,), out_shape=(jax.ShapeDtypeStruc...]
    squeeze x0 -> x1, local copies, waits for them, and re-layouts: none -> 3.41 us  [shards(): return (row_loss.reshape(rows), grads[IMG], grads[TXT])]
    unnamed x6 -> x4, local copies, waits for them, and re-layouts: 5.95 us -> 2.95 us
where the time goes in v2:
time: 109 us; the launch traced here: 108 us
  Pallas kernels  99.5 us (91%)
  local copies, waits for them, and re-layouts  6.36 us (6%)
  between operations  1.94 us (2%)
    pallas_call x1, Pallas kernels, shards(): pl.pallas_call(functools.partial(exchange, n, chunk), out_shape=(jax.Shap...  99.5 us
    squeeze x1, local copies, waits for them, and re-layouts, shards(): return (row_loss.reshape(rows), grads[IMG], grads[TXT])  3.41 us
    unnamed x4, local copies, waits for them, and re-layouts  2.95 us

profile of v2, /device:TPU:1, one launch (start us, length us, event | category | flops | bytes accessed | tf_op | source)
XLA Modules:
  0.0 108.4 jit_solution(7478416652772428218)
XLA Ops:
  1.9 0.0 copy-start
  1.9 1.5 %copy-done = bf16[768,1152]{1,0:T(8,128)(2,1)S(1)} copy-done((bf16[768,1152]{1,0:T(8,128)(2,1)S(1)}, bf16[768,1152]{1,0:T(8,128)(2,1)}, u32[]{:S(2)}) %copy-start) | copy-done | bytes 1769496
  3.4 0.0 copy-start.1
  3.4 1.5 %copy-done.1 = bf16[768,1152]{1,0:T(8,128)(2,1)S(1)} copy-done((bf16[768,1152]{1,0:T(8,128)(2,1)S(1)}, bf16[768,1152]{1,0:T(8,128)(2,1)}, u32[]{:S(2)}) %copy-start.1) | copy-done | bytes 1769496
  4.9 99.5 %shard_map.67 = (f32[2,768,1152]{2,1,0:T(8,128)S(1)}, f32[6,1,128]{2,1,0:T(1,128)S(1)}) custom-call(f32[1]{0:T(128)S(6)} %copy.7.scale_ref, f32[1]{0:T(128)S(6)} %copy.8.bias_ref, bf16[768,1152]{1,0:T(8,128)(2,1)S(1)} %copy-done, bf16[768,1152]{1,0:T(8,128)(2,1)S(1)} %copy-done.1), custom_call_target="tpu_custom_call" | custom-call | flops 14948499456 | bytes 10616832 | tf_op jit(solution)/shard_map/pallas_call | solution.py:186
  104.3 3.4 %slice_bitcast_fusion = (f32[768,1152]{1,0:T(8,128)}, f32[768,1152]{1,0:T(8,128)}) fusion(f32[2,768,1152]{2,1,0:T(8,128)S(1)} %get-tuple-element.6), kind=kLoop, calls=%fused_computation | loop fusion | bytes 14155776 | tf_op jit(solution)/shard_map/squeeze | solution.py:208
  107.8 0.6 reduce
Async XLA Ops:
  1.9 1.5 %copy-start = (bf16[768,1152]{1,0:T(8,128)(2,1)S(1)}, bf16[768,1152]{1,0:T(8,128)(2,1)}, u32[]{:S(2)}) copy-start(bf16[768,1152]{1,0:T(8,128)(2,1)} %img_hbm.1) | copy-start | bytes 5308420
  3.4 1.5 %copy-start.1 = (bf16[768,1152]{1,0:T(8,128)(2,1)S(1)}, bf16[768,1152]{1,0:T(8,128)(2,1)}, u32[]{:S(2)}) copy-start(bf16[768,1152]{1,0:T(8,128)(2,1)} %txt_hbm.1) | copy-start | bytes 5308420

commit v3 on v2

--- a/solution.py
+++ b/solution.py
@@ -26,11 +26,12 @@
     return jnp.dot(left, right, preferred_element_type=jnp.float32)
 
 
-def terms(x):
-    e = jnp.exp(-jnp.abs(x))
-    loss = jnp.maximum(x, 0.0) + jnp.log1p(e)
-    sig = jnp.where(x >= 0.0, 1.0, e) / (1.0 + e)
-    return loss, sig
+def sigmoid(x, e):
+    return jnp.where(x >= 0.0, 1.0, e) / (1.0 + e)
+
+
+def softplus(x, e):
+    return jnp.maximum(x, 0.0) + jnp.log1p(e)
 
 
 def exchange(n, chunk, scale_ref, bias_ref, img_hbm, txt_hbm, acc, row_out,
@@ -119,19 +120,26 @@
         row = lax.broadcasted_iota(jnp.int32, logits.shape, 0)
         col = lax.broadcasted_iota(jnp.int32, logits.shape, 1) + c * chunk
         flip = jnp.where(row == col, -1.0, 1.0).astype(jnp.float32)
-        part, sig = terms(flip * logits)
-        coef = (scale * flip * sig).astype(jnp.bfloat16)
-        loss[IMG] += part
+        x = flip * logits
+        e = jnp.exp(-jnp.abs(x))
+        loss[...] += softplus(x, e)
+        coef = (scale * flip * sigmoid(x, e)).astype(jnp.bfloat16)
         acc[IMG] += dot(coef, text)
         acc[TXT, span(c), :] = lax.dot_general(
             coef, low[IMG], (((0,), (0,)), ((), ())), preferred_element_type=jnp.float32)
 
+    each(lambda c: direct_two(c).start())
+
     def foreign(kind, dist, c):
         block = far[kind, dist, span(c), :]
         mine = 1 - kind
-        part, sig = terms(scale * dot_t(low[mine], block) + bias)
-        loss[mine] += part
-        acc[mine] += dot((scale * sig).astype(jnp.bfloat16), block)
+        x = scale * dot_t(low[mine], block) + bias
+        e = jnp.exp(-jnp.abs(x))
+
+        @pl.when(kind == TXT)
+        def _():
+            loss[...] += softplus(x, e)
+        acc[mine] += dot((scale * sigmoid(x, e)).astype(jnp.bfloat16), block)
 
     def take(kind, dist, c):
         arrived(kind, dist, c)
@@ -147,7 +155,6 @@
 
     each(lambda c: take(1 - parity, 0, c))
 
-    each(lambda c: direct_two(c).start())
     lag = count // 2
 
     @each
@@ -167,7 +174,7 @@
 
     @each
     def _(c):
-        lanes = jnp.sum(loss[IMG, span(c), :].T, axis=0, keepdims=True)
+        lanes = jnp.sum(loss[span(c), :].T, axis=0, keepdims=True)
         row_out[c] = lanes / (3 * rows)
 
     @each
@@ -178,11 +185,13 @@
 
 def shards(n, image_embed, text_embed, logit_scale, logit_bias):
     rows, width = image_embed.shape
-    chunk = 128
+    chunk = 256
     count = rows // chunk
     vmem = pl.BlockSpec(memory_space=pltpu.VMEM)
     smem = pl.BlockSpec(memory_space=pltpu.SMEM)
     hbm = pl.BlockSpec(memory_space=pltpu.HBM)
+    image_embed = pltpu.with_memory_space_constraint(image_embed, pltpu.HBM)
+    text_embed = pltpu.with_memory_space_constraint(text_embed, pltpu.HBM)
     grads, row_loss = pl.pallas_call(
         functools.partial(exchange, n, chunk),
         out_shape=(jax.ShapeDtypeStruct((2, rows, width), jnp.float32),
@@ -194,7 +203,7 @@
             pltpu.VMEM((2, rows, width), jnp.bfloat16),
             pltpu.VMEM((2, 2, rows, width), jnp.bfloat16),
             pltpu.VMEM((2, rows, 1), jnp.float32),
-            pltpu.VMEM((2, rows, chunk), jnp.float32),
+            pltpu.VMEM((rows, chunk), jnp.float32),
             pltpu.SemaphoreType.DMA((2, count)),
             pltpu.SemaphoreType.DMA((4, count)),
             pltpu.SemaphoreType.DMA((2, 2, count)),

time: 109 us -> 105 us (0.963)
  local copies, waits for them, and re-layouts: 6.36 us -> 4.02 us
  Pallas kernels: 99.5 us -> 97.4 us
    unnamed x4 -> x0, local copies, waits for them, and re-layouts: 2.95 us -> none
    pallas_call x1, Pallas kernels: 99.5 us -> 97.4 us  [shards(): pl.pallas_call(functools.partial(exchange, n, chunk), out_shape=(jax.Shap...]
where the time goes in v3:
time: 105 us; the launch traced here: 103 us
  Pallas kernels  97.4 us (93%)
  local copies, waits for them, and re-layouts  4.02 us (4%)
  between operations  1.93 us (2%)
    pallas_call x1, Pallas kernels, shards(): pl.pallas_call(functools.partial(exchange, n, chunk), out_shape=(jax.Shap...  97.4 us
    squeeze x1, local copies, waits for them, and re-layouts, shards(): return (row_loss.reshape(rows), grads[IMG], grads[TXT])  3.41 us

profile of v3, /device:TPU:1, one launch (start us, length us, event | category | flops | bytes accessed | tf_op | source)
XLA Modules:
  0.0 103.4 jit_solution(15928461320228551938)
XLA Ops:
  1.9 97.4 %shard_map.67 = (f32[2,768,1152]{2,1,0:T(8,128)S(1)}, f32[3,1,256]{2,1,0:T(1,128)S(1)}) custom-call(f32[1]{0:T(128)S(6)} %copy.7.scale_ref, f32[1]{0:T(128)S(6)} %copy.8.bias_ref, bf16[768,1152]{1,0:T(8,128)(2,1)} %img_hbm.1, bf16[768,1152]{1,0:T(8,128)(2,1)} %txt_hbm.1), custom_call_target="tpu_custom_call" | custom-call | flops 14948499456 | bytes 10616832 | tf_op jit(solution)/shard_map/pallas_call | solution.py:195
  99.3 3.4 %slice_bitcast_fusion = (f32[768,1152]{1,0:T(8,128)}, f32[768,1152]{1,0:T(8,128)}) fusion(f32[2,768,1152]{2,1,0:T(8,128)S(1)} %get-tuple-element.6), kind=kLoop, calls=%fused_computation | loop fusion | bytes 14155776 | tf_op jit(solution)/shard_map/squeeze | solution.py:217
  102.8 0.6 reshape.9
  (1 shorter events, 0.0 us)

commit v4 on v3

--- a/solution.py
+++ b/solution.py
@@ -73,11 +73,11 @@
     def arrived(kind, dist, c):
         copy(far.at[kind, dist, span(c), :], kind, dist, 0, c, at(1)).wait_recv()
 
-    def each(body, low_c=0, high_c=count):
+    def each(body):
         def step(c, carry):
             body(c)
             return carry
-        lax.fori_loop(low_c, high_c, step, 0)
+        lax.fori_loop(0, count, step, 0)
 
     barrier = pltpu.get_barrier_semaphore()
     for step in (1, -1, 2, -2):
@@ -103,6 +103,7 @@
     def _(c):
         text_one(c).start()
         image_one(c).start()
+        direct_two(c).start()
 
         @pl.when(c + 1 < count)
         def _():
@@ -128,8 +129,6 @@
         acc[TXT, span(c), :] = lax.dot_general(
             coef, low[IMG], (((0,), (0,)), ((), ())), preferred_element_type=jnp.float32)
 
-    each(lambda c: direct_two(c).start())
-
     def foreign(kind, dist, c):
         block = far[kind, dist, span(c), :]
         mine = 1 - kind
@@ -155,22 +154,22 @@
 
     each(lambda c: take(1 - parity, 0, c))
 
-    lag = count // 2
-
     @each
     def _(c):
         arrived(parity, 0, c)
         relay(c).start()
         foreign(parity, 0, c)
 
-        @pl.when(c >= lag)
+        @pl.when(c >= 1)
         def _():
-            take(parity, 1, c - lag)
-
-    each(lambda c: take(1 - parity, 1, c))
+            take(parity, 1, c - 1)
+            take(1 - parity, 1, c - 1)
+
+    last = count - 1
+    take(parity, 1, last)
+    finish(1 - parity)
+    take(1 - parity, 1, last)
     finish(parity)
-    each(lambda c: take(parity, 1, c), count - lag)
-    finish(1 - parity)
 
     @each
     def _(c):
@@ -185,7 +184,7 @@
 
 def shards(n, image_embed, text_embed, logit_scale, logit_bias):
     rows, width = image_embed.shape
-    chunk = 256
+    chunk = 128
     count = rows // chunk
     vmem = pl.BlockSpec(memory_space=pltpu.VMEM)
     smem = pl.BlockSpec(memory_space=pltpu.SMEM)

time: 105 us -> 101 us (0.962); the launches traced: 103 us -> 101 us
  Pallas kernels: 97.4 us -> 95.1 us
    pallas_call x1, Pallas kernels: 97.4 us -> 95.1 us  [shards(): pl.pallas_call(functools.partial(exchange, n, chunk), out_shape=(jax.Shap...]
where the time goes in v4:
time: 101 us
  Pallas kernels  95.1 us (94%)
  local copies, waits for them, and re-layouts  3.41 us (3%)
  between operations  1.93 us (2%)
    pallas_call x1, Pallas kernels, shards(): pl.pallas_call(functools.partial(exchange, n, chunk), out_shape=(jax.Shap...  95.1 us
    squeeze x1, local copies, waits for them, and re-layouts, shards(): return (row_loss.reshape(rows), grads[IMG], grads[TXT])  3.41 us

profile of v4, /device:TPU:1, one launch (start us, length us, event | category | flops | bytes accessed | tf_op | source)
XLA Modules:
  0.0 101.0 jit_solution(671703042435932574)
XLA Ops:
  1.9 95.1 %shard_map.67 = (f32[2,768,1152]{2,1,0:T(8,128)S(1)}, f32[6,1,128]{2,1,0:T(1,128)S(1)}) custom-call(f32[1]{0:T(128)S(6)} %copy.7.scale_ref, f32[1]{0:T(128)S(6)} %copy.8.bias_ref, bf16[768,1152]{1,0:T(8,128)(2,1)} %img_hbm.1, bf16[768,1152]{1,0:T(8,128)(2,1)} %txt_hbm.1), custom_call_target="tpu_custom_call" | custom-call | flops 14948499456 | bytes 10616832 | tf_op jit(solution)/shard_map/pallas_call | solution.py:194
  97.0 3.4 %slice_bitcast_fusion = (f32[768,1152]{1,0:T(8,128)}, f32[768,1152]{1,0:T(8,128)}) fusion(f32[2,768,1152]{2,1,0:T(8,128)S(1)} %get-tuple-element.6), kind=kLoop, calls=%fused_computation | loop fusion | bytes 14155776 | tf_op jit(solution)/shard_map/squeeze | solution.py:216
  100.4 0.6 reduce
